TPU v7x, 128 devices: a whole 4x4x4 slice. The times are simulated.
128 devices in a mesh: days: 8 (over z, y_lo), space: 16 (over y_hi, x, core).
Axes of the slice: x: 4, y: 4 (y_hi: 2, y_lo: 2; y = y_hi * 2 + y_lo), z: 4, core: 2. Of those that a mesh axis runs over, the one named last changes fastest.
Arguments:
- targets: bfloat16 [1536, 4, 256, 128], P('days', None, 'space'), may hold values from -16 to 16, as said below
- archive: bfloat16 [384, 4, 256, 128], P('days', None, 'space'), may hold values from -6 to 6, as said below
- archive_fine: bfloat16 [384, 512, 256], P('days', 'space'), may hold values from -6 to 6
Outputs:
- downscaled: bfloat16 [1536, 512, 256], P('days', 'space')
Inputs may be any that keep to these rules, and one draw needn't show every extreme that they name: `targets`: anomalies of the four fields. `archive`: anomalies of the four fields.
All inputs are finite; a program needn't handle non-finite values.
Results may differ from a plain program's by a relative error of at most 0.006.
Values may be sent and summed in bfloat16 or wider, within the bound.
A program may use at most 192 MiB of HBM per device.

v0:
```python
import jax
import jax.numpy as jnp
from jax import lax
from jax.sharding import PartitionSpec as P

CH = 4
BLOCK = 16
RIM = 8
COLS = 128


def with_halo(cells, sides, width):
    for axis, dim in sides:
        count = lax.axis_size(axis)
        ends = count - 1
        head = lax.slice_in_dim(cells, 0, width, axis=dim)
        tail = lax.slice_in_dim(cells, cells.shape[dim] - width, cells.shape[dim], axis=dim)
        cells = jnp.concatenate(
            [
                lax.ppermute(tail, axis, [(i, (i + 1) % count) for i in range(ends)]),
                cells,
                lax.ppermute(head, axis, [((i + 1) % count, i) for i in range(ends)]),
            ],
            axis=dim,
        )
    return cells


def windows(cells):
    block_count = COLS // BLOCK
    day_count = cells.shape[0]
    padded = jnp.pad(cells, ((0, 0), (0, 0), (0, 0), (RIM, RIM)))
    split = padded.reshape(day_count, CH, 2 * BLOCK, block_count + 1, BLOCK)
    joined = jnp.concatenate([split[..., :block_count, :], split[..., 1:, :]], axis=-1)
    return jnp.transpose(joined, (0, 3, 1, 2, 4)).reshape(
        day_count, block_count, CH * 4 * BLOCK * BLOCK
    )


def fine_layout(fine_rows):
    block_count = COLS // BLOCK
    day_count = fine_rows.shape[0]
    split = fine_rows.reshape(day_count, 2 * BLOCK, block_count, 2 * BLOCK)
    return jnp.transpose(split, (0, 2, 1, 3)).reshape(day_count, block_count, 4 * BLOCK * BLOCK)


def absorb(running, target_feat, archive_feat, fine_rows):
    peak_now, weight_sum, numerator = running
    scores = (
        jnp.einsum("tbf,abf->bta", target_feat, archive_feat, preferred_element_type=jnp.float32)
        / 32.0
    )
    peak_next = jnp.maximum(peak_now, jnp.max(scores, axis=-1))
    weights = jnp.exp(scores - peak_next[..., None])
    weight_sum = jnp.sum(weights, axis=-1)
    added = jnp.einsum(
        "bta,abk->btk",
        weights.astype(jnp.bfloat16),
        fine_layout(fine_rows),
        preferred_element_type=jnp.float32,
    )
    numerator = added
    return (peak_next, weight_sum, numerator)


def on_device(targets, archive, archive_fine):
    block_count = COLS // BLOCK
    day_count = targets.shape[0]
    target_rimmed = with_halo(targets, (("space", 2),), 8)
    target_feat = windows(target_rimmed)
    start_state = (
        jnp.full((block_count, day_count), -1e30, jnp.float32),
        jnp.zeros((block_count, day_count), jnp.float32),
        jnp.zeros((block_count, day_count, 4 * BLOCK * BLOCK), jnp.float32),
    )
    every_day = lax.all_gather(archive, "days", axis=0, tiled=True)
    every_rimmed = with_halo(every_day, (("space", 2),), 8)
    final_state = absorb(
        start_state,
        target_feat,
        windows(every_rimmed),
        lax.all_gather(archive_fine, "days", axis=0, tiled=True),
    )
    peak_now, weight_sum, numerator = final_state
    result = (numerator / weight_sum[..., None]).astype(jnp.bfloat16)
    result = result.reshape(block_count, day_count, 2 * BLOCK, 2 * BLOCK)
    return jnp.transpose(result, (1, 2, 0, 3)).reshape(day_count, 2 * BLOCK, 2 * COLS)


def solution(mesh):
    return jax.shard_map(
        on_device,
        mesh=mesh,
        in_specs=(
            P("days", None, "space", None),
            P("days", None, "space", None),
            P("days", "space", None),
        ),
        out_specs=P("days", "space", None),
        check_vma=False,
    )
```

profile of v0, /device:TPU:1, one launch (start us, length us, event | category | flops | bytes accessed | tf_op | source)
XLA Modules:
  0.0 448.9 jit_solution(13888177391788751706)
XLA Ops:
  6.5 0.0 copy-start.1
  6.5 0.0 all-gather.3.cloned.1.call-start
  6.5 0.7 all-gather.3.cloned.1.call-update
  7.3 0.0 all-gather.5.cloned.1.call-start
  7.3 0.7 all-gather.5.cloned.1.call-update
  8.0 4.1 fusion.21
  12.1 4.5 %collective-permute-start = (bf16[192,4,8,128]{3,2,1,0:T(8,128)(2,1)}, bf16[192,4,8,128]{3,2,1,0:T(8,128)(2,1)}, u32[]{:S(2)}, u32[]{:S(2)}) collective-permute-start(bf16[192,4,8,128]{3,2,1,0:T(8,128)(2,1)} %get-tuple-element.11), channel_id=1, source_target_pairs={{0,1},{1,2},{2,3},{3,4},{4,5},{5,6},{6,7},{7,8},{8,9},{9,10},{10,1... | collective-permute-start | bytes 4718600 | tf_op jit(solution)/shard_map/ppermute | solution.py:20
  16.6 1.9 collective-permute-start.1
  18.5 0.0 copy-done.1
  18.5 5.0 %copy.25 = bf16[192,4,16,128]{0,3,2,1:T(8,128)(2,1)} copy(bf16[192,4,16,128]{3,2,1,0:T(8,128)(2,1)S(1)} %copy-done.1) | data formatting | bytes 6291456 | tf_op args[0]
  23.6 10.7 %collective-permute-done = bf16[192,4,8,128]{3,2,1,0:T(8,128)(2,1)} collective-permute-done((bf16[192,4,8,128]{3,2,1,0:T(8,128)(2,1)}, bf16[192,4,8,128]{3,2,1,0:T(8,128)(2,1)}, u32[]{:S(2)}, u32[]{:S(2)}) %collective-permute-start) | collective-permute-done | bytes 1572896 | tf_op jit(solution)/shard_map/ppermute | solution.py:20
  34.3 2.8 copy.24
  37.1 1.9 collective-permute-done.1
  38.9 4.2 copy.26
  43.1 115.4 %all-gather.3.cloned.1.call-done = bf16[384,4,16,128]{3,2,1,0:T(8,128)(2,1)} async-done(((bf16[48,4,16,128]{3,2,1,0:T(8,128)(2,1)}), bf16[384,4,16,128]{3,2,1,0:T(8,128)(2,1)}) %all-gather.3.cloned.1.call-update) | async-done | bytes 6291472 | tf_op jit(solution)/shard_map/all_gather | solution.py:76
  158.5 9.1 %copy.28 = bf16[384,4,16,128]{0,3,2,1:T(8,128)(2,1)} copy(bf16[384,4,16,128]{3,2,1,0:T(8,128)(2,1)} %all-gather.3.cloned.1.call-done) | data formatting | bytes 12582912 | tf_op jit(solution)/shard_map/all_gather | solution.py:76
  167.5 0.0 copy-start
  167.5 0.0 copy-start.2
  167.5 7.1 %fusion.20 = (bf16[384,4,8,128]{0,3,2,1:T(8,128)(2,1)}, bf16[384,4,8,128]{0,3,2,1:T(8,128)(2,1)}) fusion(bf16[384,4,16,128]{0,3,2,1:T(8,128)(2,1)} %copy.28), kind=kLoop, calls=%fused_computation.29 | loop fusion | bytes 12582912 | tf_op jit(solution)/shard_map/slice | solution.py:17
  174.6 1.9 collective-permute-start.2
  176.6 4.2 collective-permute-start.3
  180.8 0.0 copy-done
  180.8 0.0 copy-done.2
  180.8 1.7 fusion.11
  182.5 2.5 fusion.19
  185.0 3.9 maximum_bitcast_fusion.1
  188.9 6.9 %copy.27 = bf16[192,8,4,32,32]{0,4,3,2,1:T(8,128)(2,1)} copy(bf16[192,8,4,32,32]{0,4,1,3,2:T(8,128)(2,1)S(1)} %maximum_bitcast_fusion.1) | data formatting | bytes 25165824 | tf_op jit(solution)/shard_map/transpose | solution.py:35
  195.8 123.0 %all-gather.5.cloned.1.call-done = bf16[384,32,256]{2,1,0:T(8,128)(2,1)} async-done(((bf16[48,32,256]{2,1,0:T(8,128)(2,1)}), bf16[384,32,256]{2,1,0:T(8,128)(2,1)}) %all-gather.5.cloned.1.call-update) | async-done | bytes 6291472 | tf_op jit(solution)/shard_map/all_gather | solution.py:82
  318.8 9.1 %copy.34 = bf16[384,32,256]{0,2,1:T(8,128)(2,1)} copy(bf16[384,32,256]{2,1,0:T(8,128)(2,1)} %all-gather.5.cloned.1.call-done) | data formatting | bytes 12582912 | tf_op jit(solution)/shard_map/all_gather | solution.py:82
  327.9 0.0 slice-start
  327.9 0.0 slice-start.1
  327.9 6.5 %copy.35 = bf16[384,8,32,32]{0,3,2,1:T(8,128)(2,1)} copy(bf16[384,8,32,32]{0,3,1,2:T(8,128)(2,1)} %bitcast.25) | data formatting | bytes 12582912 | tf_op jit(solution)/shard_map/transpose | solution.py:44
  334.3 0.0 collective-permute-done.2
  334.4 0.0 collective-permute-done.3
  334.4 0.0 slice-done
  334.4 0.0 slice-done.1
  334.4 8.2 %fusion.6 = bf16[384,4,32,144]{0,3,2,1:T(8,128)(2,1)S(1)} fusion(bf16[384,4,8,128]{0,3,2,1:T(8,128)(2,1)} %collective-permute-done.3, bf16[384,4,16,128]{0,3,2,1:T(8,128)(2,1)S(1)} %bitcast.24, bf16[384,4,8,128]{0,3,2,1:T(8,128)(2,1)} %collective-permute-done.2), kind=kLoop, calls=%fused_computation.12 | loop fusion | flops 84934656 | bytes 26738688 | tf_op jit(solution)/shard_map/concatenate | solution.py:18
  342.6 11.7 %fusion.18 = (bf16[384,4,32,8,16]{0,4,3,2,1:T(8,128)(2,1)}, bf16[384,4,32,8,16]{0,4,3,2,1:T(8,128)(2,1)}) fusion(bf16[384,4,32,9,16]{0,4,3,2,1:T(8,128)(2,1)S(1)} %bitcast.19), kind=kLoop, calls=%fused_computation.27 | loop fusion | bytes 50331648 | tf_op jit(solution)/shard_map/slice | solution.py:34
  354.2 0.0 slice-start.2
  354.2 22.4 %maximum_bitcast_fusion = bf16[384,8,4,32,32]{0,4,1,3,2:T(8,128)(2,1)} fusion(bf16[384,4,32,8,16]{0,4,3,2,1:T(8,128)(2,1)} %get-tuple-element.6, bf16[384,4,32,8,16]{0,4,3,2,1:T(8,128)(2,1)} %get-tuple-element.5), kind=kLoop, calls=%fused_computation.5 | loop fusion | flops 50331648 | bytes 50331648 | tf_op jit(solution)/shard_map/transpose | solution.py:35
  376.6 0.0 slice-start.3
  376.6 22.6 %copy.31 = bf16[384,8,4,32,32]{0,4,3,2,1:T(8,128)(2,1)} copy(bf16[384,8,4,32,32]{0,4,1,3,2:T(8,128)(2,1)} %maximum_bitcast_fusion) | data formatting | bytes 50331648 | tf_op jit(solution)/shard_map/transpose | solution.py:35
  399.2 20.0 %multiply_reduce_fusion = (f32[8,192]{1,0:T(8,128)S(1)}, f32[8,192,384]{2,1,0:T(8,128)S(1)}) fusion(bf16[192,8,4096]{0,2,1:T(8,128)(2,1)} %bitcast.22, bf16[384,8,4096]{0,2,1:T(8,128)(2,1)} %bitcast.20), kind=kOutput, calls=%fused_computation.20 | convolution fusion | flops 4833016320 | bytes 40114176 | tf_op jit(solution)/shard_map/tbf,abf->bta/dot_general | solution.py:50
  419.2 0.8 fusion.12
  420.1 0.0 slice-done.2
  420.1 0.0 slice-done.3
  420.1 3.9 divide_convert_fusion
  424.0 6.2 %copy.37 = bf16[8,192,1024]{1,2,0:T(8,128)(2,1)} copy(bf16[8,192,1024]{2,1,0:T(8,128)(2,1)} %divide_convert_fusion) | data formatting | bytes 6291456 | tf_op jit(solution)/shard_map/convert_element_type | solution.py:85
  430.1 4.8 %copy.38 = bf16[192,32,8,32]{0,3,2,1:T(8,128)(2,1)} copy(bf16[192,32,8,32]{0,3,1,2:T(8,128)(2,1)} %bitcast.26) | data formatting | bytes 6291456 | tf_op jit(solution)/shard_map/transpose | solution.py:87
  435.0 7.1 %copy.39 = bf16[192,32,256]{2,1,0:T(8,128)(2,1)} copy(bf16[192,32,256]{0,2,1:T(8,128)(2,1)} %bitcast.27) | data formatting | bytes 6291456 | tf_op jit(solution)/shard_map/reshape | solution.py:87
  (3 shorter events, 0.0 us)
Async XLA Ops:
  6.5 12.0 %copy-start.1 = (bf16[192,4,16,128]{3,2,1,0:T(8,128)(2,1)S(1)}, bf16[192,4,16,128]{3,2,1,0:T(8,128)(2,1)}, u32[]{:S(2)}) copy-start(bf16[192,4,16,128]{3,2,1,0:T(8,128)(2,1)} %param.3) | copy-start | bytes 9437188
  6.5 151.9 %all-gather.3.cloned.1.call-start = ((), (), s32[]{:S(2)}) async-start(), calls=%async_computation | async-start | bytes 7077888 | tf_op jit(solution)/shard_map/all_gather | solution.py:76
  7.3 311.5 %all-gather.5.cloned.1.call-start = ((), (), s32[]{:S(2)}) async-start(), calls=%async_computation.1 | async-start | bytes 7077888 | tf_op jit(solution)/shard_map/all_gather | solution.py:82
  12.1 22.2 %collective-permute-start = (bf16[192,4,8,128]{3,2,1,0:T(8,128)(2,1)}, bf16[192,4,8,128]{3,2,1,0:T(8,128)(2,1)}, u32[]{:S(2)}, u32[]{:S(2)}) collective-permute-start(bf16[192,4,8,128]{3,2,1,0:T(8,128)(2,1)} %get-tuple-element.11), channel_id=1, source_target_pairs={{0,1},{1,2},{2,3},{3,4},{4,5},{5,6},{6,7},{7,8},{8,9},{9,10},{10,1... | collective-permute-start | bytes 4718600 | tf_op jit(solution)/shard_map/ppermute | solution.py:20
  16.6 22.3 %collective-permute-start.1 = (bf16[192,4,8,128]{3,2,1,0:T(8,128)(2,1)}, bf16[192,4,8,128]{3,2,1,0:T(8,128)(2,1)}, u32[]{:S(2)}, u32[]{:S(2)}) collective-permute-start(bf16[192,4,8,128]{3,2,1,0:T(8,128)(2,1)} %get-tuple-element.12), channel_id=1, source_target_pairs={{1,0},{2,1},{3,2},{4,3},{5,4},{6,5},{7,6},{8,7},{9,8},{10,9},{11,1... | collective-permute-start | bytes 4718600 | tf_op jit(solution)/shard_map/ppermute | solution.py:22
  167.5 13.3 %copy-start = (bf16[192,4,16,128]{0,3,2,1:T(8,128)(2,1)S(1)}, bf16[192,4,16,128]{0,3,2,1:T(8,128)(2,1)}, u32[]{:S(2)}) copy-start(bf16[192,4,16,128]{0,3,2,1:T(8,128)(2,1)} %copy.25) | copy-start | bytes 9437188
  167.5 13.3 %copy-start.2 = (bf16[192,4,8,128]{0,3,2,1:T(8,128)(2,1)S(1)}, bf16[192,4,8,128]{0,3,2,1:T(8,128)(2,1)}, u32[]{:S(2)}) copy-start(bf16[192,4,8,128]{0,3,2,1:T(8,128)(2,1)} %copy.26) | copy-start | bytes 4718596
  174.6 159.7 %collective-permute-start.2 = (bf16[384,4,8,128]{0,3,2,1:T(8,128)(2,1)}, bf16[384,4,8,128]{0,3,2,1:T(8,128)(2,1)}, u32[]{:S(2)}, u32[]{:S(2)}) collective-permute-start(bf16[384,4,8,128]{0,3,2,1:T(8,128)(2,1)} %get-tuple-element.9), channel_id=1, source_target_pairs={{0,1},{1,2},{2,3},{3,4},{4,5},{5,6},{6,7},{7,8},{8,9},{9,10},{10,1... | collective-permute-start | bytes 9437192 | tf_op jit(solution)/shard_map/ppermute | solution.py:20
  176.6 157.8 %collective-permute-start.3 = (bf16[384,4,8,128]{0,3,2,1:T(8,128)(2,1)}, bf16[384,4,8,128]{0,3,2,1:T(8,128)(2,1)}, u32[]{:S(2)}, u32[]{:S(2)}) collective-permute-start(bf16[384,4,8,128]{0,3,2,1:T(8,128)(2,1)} %get-tuple-element.10), channel_id=1, source_target_pairs={{1,0},{2,1},{3,2},{4,3},{5,4},{6,5},{7,6},{8,7},{9,8},{10,9},{11,1... | collective-permute-start | bytes 9437192 | tf_op jit(solution)/shard_map/ppermute | solution.py:22
  327.9 6.5 %slice-start = ((s8[6291456]{0:T(1024)(128)(4,1)}), s8[4194304]{0:T(1024)(128)(4,1)S(1)}, s32[]{:S(2)}) async-start(s8[6291456]{0:T(1024)(128)(4,1)} %bitcast.23), calls=%async_computation.2 | async-start | bytes 8388608
  327.9 6.5 %slice-start.1 = ((s8[6291456]{0:T(1024)(128)(4,1)}), s8[2097152]{0:T(1024)(128)(4,1)S(1)}, s32[]{:S(2)}) async-start(s8[6291456]{0:T(1024)(128)(4,1)} %bitcast.23), calls=%async_computation.3 | async-start | bytes 4194304
  354.2 65.8 %slice-start.2 = ((s8[6291456]{0:T(1024)(128)(4,1)}), s8[2097152]{0:T(1024)(128)(4,1)S(1)}, s32[]{:S(2)}) async-start(s8[6291456]{0:T(1024)(128)(4,1)} %bitcast.28), calls=%async_computation.4 | async-start | bytes 4194304
  376.6 43.5 %slice-start.3 = ((s8[6291456]{0:T(1024)(128)(4,1)}), s8[4194304]{0:T(1024)(128)(4,1)S(1)}, s32[]{:S(2)}) async-start(s8[6291456]{0:T(1024)(128)(4,1)} %bitcast.28), calls=%async_computation.5 | async-start | bytes 8388608
Sparse Core Ops, SparseCore 0:
  9.0 149.4 all-gather.2
  160.1 158.6 all-gather.4
where the time goes:
time: 453 us; the launch traced here: 449 us
  waiting for transfers between devices  252 us (56%)
  local copies, waits for them, and re-layouts  110 us (24%)
  other arithmetic  37 us (8%)
  matrix products  23.9 us (5%)
  between operations  13.6 us (3%)
  starting transfers between devices  12.6 us (3%)
    all_gather x1, waiting for transfers between devices, on_device(): lax.all_gather(archive_fine, 'days', axis=0, tiled=True)  123 us
    all_gather x1, waiting for transfers between devices, on_device(): every_day = lax.all_gather(archive, 'days', axis=0, tiled=True)  115 us
    transpose x2, local copies, waits for them, and re-layouts, windows(): jnp.transpose(joined, (0, 3, 1, 2, 4))  29.5 us
    transpose x2, other arithmetic, windows(): jnp.transpose(joined, (0, 3, 1, 2, 4))  26.3 us
    dot_general x1, matrix products, absorb(): jnp.einsum('tbf,abf->bta', target_feat, archive_feat, preferred_element_t...  20 us
    slice x2, local copies, waits for them, and re-layouts, windows(): split[..., :block_count, :]  14.2 us
    slice x2, local copies, waits for them, and re-layouts, with_halo(): lax.slice_in_dim(cells, cells.shape[dim] - width, cells.shape[dim], axis=...  11.2 us
    ppermute x2, waiting for transfers between devices, with_halo(): lax.ppermute(tail, axis, [(i, (i + 1) % count) for i in range(ends)])  10.7 us
  transfers between devices with their start and end apart: 6, of which 4 were waited for; matrix products, arithmetic and copies ran while one was open for 14% of the time, Pallas kernels for 0%

commit v1 on v0

v1 whole, which is shorter than its diff:
```python
import functools

import jax
import jax.numpy as jnp
import ml_dtypes
import numpy as np
from jax import lax
from jax.experimental import pallas as pl
from jax.experimental.pallas import tpu as pltpu
from jax.sharding import PartitionSpec as P

MESH = pl.DeviceIdType.MESH
BF16, F32 = jnp.bfloat16, jnp.float32

NT, NA, NB = 192, 48, 8
ALL = 8 * NA
PIECE = 16

SENDS = {
    "y": [(0, 3, 0), (0, 3, 1), (0, 3, 2), (1, 4, 0), (2, 5, 0), (1, 4, 1), (2, 5, 1)],
    "z+": [(0, 2, 0), (0, 2, 1), (0, 2, 2), (2, 6, 0), (3, 5, 2), (2, 6, 1), (5, 7, 0)],
    "z-": [(0, 1, 0), (0, 1, 1), (0, 1, 2), (1, 6, 2), (3, 4, 2), (4, 7, 2), (4, 7, 1)],
}


def swap_matrix():
    m = np.zeros((16, 16, 16, 16), np.float32)
    for r in range(16):
        for t in range(16):
            m[r, t, t, r] = 1
    return m.reshape(256, 256).astype(ml_dtypes.bfloat16)


def cell_matrix():
    m = np.zeros((8, 128, 8, 8, 16), np.float32)
    for r in range(8):
        for j in range(8):
            for q in range(16):
                m[r, (16 * j - 8 + q) % 128, j, r, q] = 1
    return m.reshape(1024, 1024).astype(ml_dtypes.bfloat16)


def fine_matrix():
    m = np.zeros((4, 8, 32, 8, 4, 32), np.float32)
    for i in range(4):
        for b in range(8):
            for q in range(32):
                m[i, b, q, b, i, q] = 1
    return m.reshape(1024, 1024).astype(ml_dtypes.bfloat16)


def dot(a, b):
    return jnp.dot(a, b, preferred_element_type=F32)


def dot_t(a, b):
    return lax.dot_general(a, b, (((1,), (1,)), ((), ())), preferred_element_type=F32)


def gather_kernel(
    tgt_hbm, arc_hbm, fin_hbm, swap_ref, cellm_hbm, finem_hbm, out_hbm,
    t_raw, a_raw, f_raw, cellm, finem, ga, gf, tf, zbuf, own, xs, xr, relay, wts, inv, res,
    lsem, osem, gsend, grecv, xsend, xrecv, rsend, rrecv,
):
    d = lax.axis_index("days")
    s = lax.axis_index("space")
    z, y = d // 2, d % 2
    partner = 2 * z + 1 - y
    to = {"y": partner, "z+": 2 * lax.rem(z + 1, 4) + y, "z-": 2 * lax.rem(z + 3, 4) + y}

    up_direct = (s != 7) & (s != 15)
    down_direct = (s != 0) & (s != 8)
    is_edge = (s == 7) | (s == 8)
    low = s < 8
    is_relay = (low & (s % 2 == 1)) | (jnp.logical_not(low) & (s % 2 == 0))
    relay_to = jnp.where(low, 8, 7)
    relay_from = jnp.where(low, 7, 8)
    quarter = (s % 8) // 2
    first_relay = jnp.where(low, 1, 8)
    last_relay = jnp.where(low, 8, 1)

    barrier = pltpu.get_barrier_semaphore()

    def greet(day, space):
        pl.semaphore_signal(barrier, inc=1, device_id=(day, space), device_id_type=MESH)

    for link in to:
        greet(to[link], s)

    @pl.when(up_direct)
    def _():
        greet(d, s + 1)

    @pl.when(down_direct)
    def _():
        greet(d, s - 1)

    @pl.when(is_relay)
    def _():
        greet(partner, relay_from)

    @pl.when(is_edge)
    def _():
        for p in range(4):
            greet(partner, last_relay + 2 * p)

    loads = [
        pltpu.make_async_copy(src, dst, lsem.at[i])
        for i, (src, dst) in enumerate(
            [(arc_hbm, a_raw), (cellm_hbm, cellm), (finem_hbm, finem), (fin_hbm, f_raw), (tgt_hbm, t_raw)]
        )
    ]
    for load in loads:
        load.start()

    swap = swap_ref[...]
    lane = lax.broadcasted_iota(jnp.int32, (1, 128), 1) % 16
    right_half = jnp.where(lane >= 8, 1.0, 0.0).astype(BF16)
    left_half = jnp.where(lane < 8, 1.0, 0.0).astype(BF16)

    def cells(src, first, days, put):
        for tb in range(days // 16):
            for cp in range(2):
                x = jnp.concatenate(
                    [src[pl.ds(first + 16 * tb, 16), 2 * cp + c].reshape(256, 128) for c in range(2)], axis=1
                )
                w = dot(swap, x).astype(BF16)
                for c in range(2):
                    for r in range(16):
                        row = ((2 * cp + c) * 2 + r // 8) * days + 16 * tb
                        zbuf[pl.ds(row, 16), pl.ds((r % 8) * 128, 128)] = w[16 * r : 16 * r + 16, 128 * c : 128 * c + 128]
        for jp in range(4):
            o = dot(zbuf[pl.ds(0, 8 * days)], cellm[:, pl.ds(256 * jp, 256)]).astype(BF16)
            for c in range(4):
                for half in range(2):
                    row = (2 * c + half) * days
                    for jj in range(2):
                        put(half, 2 * jp + jj, c, o[row : row + days, 128 * jj : 128 * jj + 128])

    bufs = (ga, gf)

    def piece(arr, slot, p):
        return bufs[arr].at[:, pl.ds(slot * NA + p * PIECE, PIECE)]

    def remote(arr, link, there, src, dst, p):
        return pltpu.make_async_remote_copy(
            src_ref=piece(arr, src, p), dst_ref=piece(arr, dst, p),
            send_sem=gsend.at[arr, dst, p], recv_sem=grecv.at[arr, dst, p],
            device_id=(there, s), device_id_type=MESH,
        )

    arrived = {(arr, 0, p) for arr in range(2) for p in range(3)}
    sent = []

    def need(arr, slot, p):
        if (arr, slot, p) not in arrived:
            arrived.add((arr, slot, p))
            remote(arr, "y", partner, slot, slot, p).wait_recv()

    def send(arr, step):
        for link in to:
            src, dst, p = SENDS[link][step]
            need(arr, src, p)
            copy = remote(arr, link, to[link], src, dst, p)
            copy.start()
            sent.append(copy)

    def halo(row, k):
        there = s + 1 if row == 0 else s - 1
        return pltpu.make_async_remote_copy(
            src_ref=xs.at[row, k], dst_ref=xr.at[row, k],
            send_sem=xsend.at[row, k, 0], recv_sem=xrecv.at[row, k, 0],
            device_id=(d, there), device_id_type=MESH,
        )

    def halo_quarter(row, k, p):
        return pltpu.make_async_remote_copy(
            src_ref=xs.at[row, k, pl.ds(2 * p, 2)], dst_ref=relay.at[k],
            send_sem=xsend.at[row, k, p], recv_sem=rrecv.at[k],
            device_id=(partner, first_relay + 2 * p), device_id_type=MESH,
        )

    def pass_on(row, k, p):
        return pltpu.make_async_remote_copy(
            src_ref=relay.at[k], dst_ref=xr.at[row, k, pl.ds(2 * p, 2)],
            send_sem=rsend.at[k], recv_sem=xrecv.at[row, k, p],
            device_id=(partner, relay_to), device_id_type=MESH,
        )

    def halo_start(k):
        for row, direct, edge in ((0, up_direct, 7), (1, down_direct, 8)):
            @pl.when(direct)
            def _():
                halo(row, k).start()

            @pl.when(s == edge)
            def _():
                for p in range(4):
                    halo_quarter(row, k, p).start()

    def halo_pass(k):
        for row in range(2):
            @pl.when(is_relay & (low if row == 0 else jnp.logical_not(low)))
            def _():
                halo_quarter(row, k, 0).wait_recv()
                pass_on(row, k, quarter).start()

    def halo_wait(k):
        for row, direct, edge in ((0, down_direct, 8), (1, up_direct, 7)):
            @pl.when(direct)
            def _():
                halo(row, k).wait_recv()

            @pl.when(s == edge)
            def _():
                for p in range(4):
                    pass_on(row, k, p).wait_recv()

    def halo_drain(k):
        for row, direct, edge in ((0, up_direct, 7), (1, down_direct, 8)):
            @pl.when(direct)
            def _():
                halo(row, k).wait_send()

            @pl.when(s == edge)
            def _():
                for p in range(4):
                    halo_quarter(row, k, p).wait_send()

        @pl.when(is_relay)
        def _():
            pass_on(0, k, quarter).wait_send()

    def scores(k):
        days = pl.ds(128 * k, 128)

        @pl.loop(0, NB)
        def _(b):
            after = lax.rem(b + 1, NB)
            upper = dot_t(tf[b], ga[b, days]) + dot_t(tf[b + 1], ga[after, days])
            lower = dot_t(tf[9 + b], ga[8 + b, days]) + dot_t(tf[10 + b], ga[8 + after, days])
            own[k, b] = upper + lower
            xs[0, k, b] = lower
            xs[1, k, b] = upper

        halo_start(k)

    loads[0].wait()
    loads[1].wait()
    for p in range(3):
        def put(half, j, c, v):
            ga[8 * half + j, pl.ds(PIECE * p, PIECE), pl.ds(128 * c, 128)] = v

        cells(a_raw, PIECE * p, PIECE, put)
        if p == 0:
            pl.semaphore_wait(
                barrier,
                3 + up_direct.astype(jnp.int32) + down_direct.astype(jnp.int32)
                + is_relay.astype(jnp.int32) + 4 * is_edge.astype(jnp.int32),
            )
        send(0, p)

    loads[2].wait()
    loads[3].wait()
    for tb in range(3):
        for half in range(2):
            x = f_raw[pl.ds(16 * tb, 16), pl.ds(16 * half, 16)].reshape(256, 256)
            w = dot(swap, x).astype(BF16)
            for r in range(16):
                g, i = (16 * half + r) // 4, r % 4
                zbuf[pl.ds(NA * g + 16 * tb, 16), pl.ds(256 * i, 256)] = w[16 * r : 16 * r + 16]
    for bp in range(4):
        o = dot(zbuf[...], finem[:, pl.ds(256 * bp, 256)]).astype(BF16)
        for bb in range(2):
            for g in range(8):
                gf[2 * bp + bb, pl.ds(0, NA), pl.ds(128 * g, 128)] = o[NA * g : NA * g + NA, 128 * bb : 128 * bb + 128]

    loads[4].wait()

    @pl.loop(0, NT // NA)
    def _(n):
        first = pl.multiple_of(n * NA, NA)
        days = pl.ds(first, NA)

        def put(half, j, c, v):
            cols = pl.ds(128 * c, 128)
            if j:
                tf[9 * half + j, days, cols] = v
            else:
                tf[9 * half, days, cols] = v * right_half
                tf[9 * half + 8, days, cols] = v * left_half

        cells(t_raw, first, NA, put)

    for row, edge in ((0, 0), (1, 15)):
        @pl.when(s == edge)
        def _():
            xr[row] = jnp.zeros(xr.shape[1:], F32)

    def need_days(arr, lo, hi):
        for slot in range(8):
            for p in range(3):
                if lo <= slot * NA + p * PIECE < hi:
                    need(arr, slot, p)

    send(0, 3)
    need_days(0, 0, 128)
    scores(0)
    send(0, 4)
    send(0, 5)
    send(0, 6)
    send(1, 0)
    halo_pass(0)
    need_days(0, 128, 256)
    scores(1)
    send(1, 1)
    send(1, 2)
    need_days(0, 256, 384)
    scores(2)
    halo_pass(1)
    send(1, 3)
    send(1, 4)
    halo_pass(2)
    send(1, 5)
    for k in range(3):
        halo_wait(k)

    @pl.loop(0, NB)
    def _(b):
        x = [(own[k, b] + xr[0, k, b] + xr[1, k, b]) * (1.0 / 32.0) for k in range(3)]
        peak = jnp.max(jnp.maximum(jnp.maximum(x[0], x[1]), x[2]), axis=1, keepdims=True)
        e = [jnp.exp(v - peak) for v in x]
        total = jnp.sum(e[0] + e[1] + e[2], axis=1, keepdims=True)
        for k in range(3):
            wts[b, :, pl.ds(128 * k, 128)] = e[k].astype(BF16)
        inv[b] = jnp.broadcast_to(1.0 / total, (NT, 128))

    send(1, 6)
    need_days(1, 0, 384)

    def store(b):
        return pltpu.make_async_copy(res.at[b], out_hbm.at[b], osem.at[b])

    @pl.loop(0, NB)
    def _(b):
        scale = jnp.concatenate([inv[b], inv[b]], axis=1)
        for n in range(4):
            cols = pl.ds(256 * n, 256)
            res[b, :, cols] = (dot(wts[b], gf[b, :, cols]) * scale).astype(BF16)
        store(b).start()

    for k in range(3):
        halo_drain(k)
    for copy in sent:
        copy.wait_send()
    for b in range(NB):
        store(b).wait()


def lay_out_kernel(res_ref, finem_ref, swap_ref, out_ref, zbuf, rows):
    for g in range(8):
        for b in range(NB):
            zbuf[pl.ds(NA * g, NA), pl.ds(128 * b, 128)] = res_ref[b, :, pl.ds(128 * g, 128)]
    for i in range(4):
        o = dot_t(zbuf[...], finem_ref[pl.ds(256 * i, 256)]).astype(BF16)
        for g in range(8):
            rows[4 * g + i] = o[NA * g : NA * g + NA]
    for tb in range(3):
        for half in range(2):
            x = rows[pl.ds(16 * half, 16), pl.ds(16 * tb, 16)].reshape(256, 256)
            o = dot(swap_ref[...], x).astype(BF16)
            out_ref[pl.ds(16 * tb, 16), pl.ds(16 * half, 16)] = o.reshape(16, 16, 256)


def on_device(targets, archive, archive_fine):
    swap = jnp.asarray(swap_matrix())
    cellm = jnp.asarray(cell_matrix())
    finem = jnp.asarray(fine_matrix())
    hbm = pl.BlockSpec(memory_space=pl.ANY)
    vmem = pl.BlockSpec(memory_space=pltpu.VMEM)
    dma = pltpu.SemaphoreType.DMA
    res = pl.pallas_call(
        gather_kernel,
        out_shape=jax.ShapeDtypeStruct((NB, NT, 1024), BF16),
        in_specs=[hbm, hbm, hbm, vmem, hbm, hbm],
        out_specs=hbm,
        scratch_shapes=[
            pltpu.VMEM((NT, 4, 16, 128), BF16),
            pltpu.VMEM((NA, 4, 16, 128), BF16),
            pltpu.VMEM((NA, 32, 256), BF16),
            pltpu.VMEM((1024, 1024), BF16),
            pltpu.VMEM((1024, 1024), BF16),
            pltpu.VMEM((16, ALL, 512), BF16),
            pltpu.VMEM((NB, ALL, 1024), BF16),
            pltpu.VMEM((18, NT, 512), BF16),
            pltpu.VMEM((8 * NA, 1024), BF16),
            pltpu.VMEM((3, NB, NT, 128), F32),
            pltpu.VMEM((2, 3, NB, NT, 128), F32),
            pltpu.VMEM((2, 3, NB, NT, 128), F32),
            pltpu.VMEM((3, 2, NT, 128), F32),
            pltpu.VMEM((NB, NT, ALL), BF16),
            pltpu.VMEM((NB, NT, 128), F32),
            pltpu.VMEM((NB, NT, 1024), BF16),
            dma((5,)), dma((NB,)), dma((2, 8, 3)), dma((2, 8, 3)),
            dma((2, 3, 4)), dma((2, 3, 4)), dma((3,)), dma((3,)),
        ],
        compiler_params=pltpu.CompilerParams(
            collective_id=0, has_side_effects=True, vmem_limit_bytes=60 << 20
        ),
        cost_estimate=pl.CostEstimate(flops=6_000_000_000, bytes_accessed=16_000_000, transcendentals=600_000),
    )(targets, archive, archive_fine, swap, cellm, finem)
    return pl.pallas_call(
        lay_out_kernel,
        grid=(NT // NA,),
        out_shape=jax.ShapeDtypeStruct((NT, 32, 256), BF16),
        in_specs=[
            pl.BlockSpec((NB, NA, 1024), lambda n: (0, n, 0)),
            pl.BlockSpec((1024, 1024), lambda n: (0, 0)),
            pl.BlockSpec((256, 256), lambda n: (0, 0)),
        ],
        out_specs=pl.BlockSpec((NA, 32, 256), lambda n: (n, 0, 0)),
        scratch_shapes=[pltpu.VMEM((8 * NA, 1024), BF16), pltpu.VMEM((32, NA, 256), BF16)],
        compiler_params=pltpu.CompilerParams(vmem_limit_bytes=40 << 20),
        cost_estimate=pl.CostEstimate(flops=4_000_000_000, bytes_accessed=8_000_000, transcendentals=0),
    )(res, finem, swap)


def solution(mesh):
    return jax.shard_map(
        on_device,
        mesh=mesh,
        in_specs=(
            P("days", None, "space", None),
            P("days", None, "space", None),
            P("days", "space", None),
        ),
        out_specs=P("days", "space", None),
        check_vma=False,
    )
```

time: 453 us -> 108 us (0.24)
  waiting for transfers between devices: 252 us -> 0 us
  local copies, waits for them, and re-layouts: 110 us -> 1.89 us
  Pallas kernels: 0 us -> 104 us
  other arithmetic: 37 us -> 0 us
  matrix products: 23.9 us -> 0 us
  between operations: 13.6 us -> 0.03 us
  starting transfers between devices: 12.6 us -> 0 us
    all_gather x2 -> x0, waiting for transfers between devices: 238 us -> none  [the longest x1 123 us: on_device(): lax.all_gather(archive_fine, 'days', axis=0, tiled=True)]
    pallas_call x0 -> x2, Pallas kernels: none -> 104 us  [the longest x1 97.2 us: on_device(): pl.pallas_call(gather_kernel, out_shape=jax.ShapeDtypeStruct((NB, NT, 102...]
    transpose x4 -> x0, local copies, waits for them, and re-layouts: 40.8 us -> none  [the longest x2 29.5 us: windows(): jnp.transpose(joined, (0, 3, 1, 2, 4))]
    transpose x2 -> x0, other arithmetic: 26.3 us -> none  [windows(): jnp.transpose(joined, (0, 3, 1, 2, 4))]
    slice x4 -> x0, local copies, waits for them, and re-layouts: 25.3 us -> none  [the longest x2 14.2 us: windows(): split[..., :block_count, :]]
    dot_general x2 -> x0, matrix products: 23.9 us -> none  [the longest x1 20 us: absorb(): jnp.einsum('tbf,abf->bta', target_feat, archive_feat, preferred_element_t...]
    all_gather x2 -> x0, local copies, waits for them, and re-layouts: 18.2 us -> none  [the longest x1 9.08 us: on_device(): every_day = lax.all_gather(archive, 'days', axis=0, tiled=True)]
    ppermute x4 -> x0, waiting for transfers between devices: 12.6 us -> none  [the longest x2 10.7 us: with_halo(): lax.ppermute(tail, axis, [(i, (i + 1) % count) for i in range(ends)])]
  transfers between devices with their start and end apart: 6 -> 0, of which waited for: 4 -> 0; matrix products, arithmetic and copies ran while one was open for 14% -> 0% of each run, Pallas kernels for 0% -> 0%
where the time goes in v1:
time: 108 us; the launch traced here: 106 us
  Pallas kernels  104 us (96%)
  local copies, waits for them, and re-layouts  1.89 us (2%)
    pallas_call x1, Pallas kernels, on_device(): pl.pallas_call(gather_kernel, out_shape=jax.ShapeDtypeStruct((NB, NT, 102...  97.2 us
    pallas_call x1, Pallas kernels, on_device(): pl.pallas_call(lay_out_kernel, grid=(NT // NA,), out_shape=jax.ShapeDtype...  6.48 us

profile of v1, /device:TPU:1, one launch (start us, length us, event | category | flops | bytes accessed | tf_op | source)
XLA Modules:
  0.0 105.6 jit_solution(3133001076739888699)
XLA Ops:
  0.0 0.0 copy-start
  0.0 0.0 copy-start.1
  0.0 97.2 %shard_map.64.res_ref = bf16[8,192,1024]{2,1,0:T(8,128)(2,1)} custom-call(bf16[192,4,16,128]{3,2,1,0:T(8,128)(2,1)} %tgt_hbm.1, bf16[48,4,16,128]{3,2,1,0:T(8,128)(2,1)} %arc_hbm.1, bf16[48,32,256]{2,1,0:T(8,128)(2,1)} %fin_hbm.1, bf16[256,256]{1,0:T(8,128)(2,1)} %constant.6.clone.swap_ref, bf16[1024,1024]{1,0:T(8,128)(2,1)} %constant.7.clone.cellm_hbm, ...), custom_call_target="tpu_custom_call" | custom-call | flops 6000000000 | bytes 16000000 | tf_op jit(solution)/shard_map/pallas_call | solution.py:382
  97.2 0.0 copy-done
  97.2 0.0 copy-done.1
  97.2 0.0 copy-start.2
  97.2 1.9 %copy-done.2 = bf16[8,192,1024]{2,1,0:T(8,128)(2,1)S(1)} copy-done((bf16[8,192,1024]{2,1,0:T(8,128)(2,1)S(1)}, bf16[8,192,1024]{2,1,0:T(8,128)(2,1)}, u32[]{:S(2)}) %copy-start.2) | copy-done | bytes 3145752
  99.1 6.5 %shard_map.65 = bf16[192,32,256]{2,1,0:T(8,128)(2,1)} custom-call(bf16[8,192,1024]{2,1,0:T(8,128)(2,1)S(1)} %copy-done.2, bf16[1024,1024]{1,0:T(8,128)(2,1)S(1)} %copy-done, bf16[256,256]{1,0:T(8,128)(2,1)S(1)} %copy-done.1), custom_call_target="tpu_custom_call" | custom-call | flops 4000000000 | bytes 8000000 | tf_op jit(solution)/shard_map/pallas_call | solution.py:412
Async XLA Ops:
  0.0 97.2 %copy-start = (bf16[1024,1024]{1,0:T(8,128)(2,1)S(1)}, bf16[1024,1024]{1,0:T(8,128)(2,1)}, u32[]{:S(2)}) copy-start(bf16[1024,1024]{1,0:T(8,128)(2,1)} %constant.8.clone.finem_hbm.finem_ref) | copy-start | bytes 6291460
  0.0 97.2 %copy-start.1 = (bf16[256,256]{1,0:T(8,128)(2,1)S(1)}, bf16[256,256]{1,0:T(8,128)(2,1)}, u32[]{:S(2)}) copy-start(bf16[256,256]{1,0:T(8,128)(2,1)} %constant.6.clone.swap_ref) | copy-start | bytes 393220
  97.2 1.9 %copy-start.2 = (bf16[8,192,1024]{2,1,0:T(8,128)(2,1)S(1)}, bf16[8,192,1024]{2,1,0:T(8,128)(2,1)}, u32[]{:S(2)}) copy-start(bf16[8,192,1024]{2,1,0:T(8,128)(2,1)} %shard_map.64.res_ref) | copy-start | bytes 9437188

commit v2 on v1

v2 whole, which is shorter than its diff:
```python
import functools

import jax
import jax.numpy as jnp
import ml_dtypes
import numpy as np
from jax import lax
from jax.experimental import pallas as pl
from jax.experimental.pallas import tpu as pltpu
from jax.sharding import PartitionSpec as P

MESH = pl.DeviceIdType.MESH
BF16, F32 = jnp.bfloat16, jnp.float32

NT, NA, NB = 192, 48, 8
ALL = 8 * NA

HEAD = [
    (0, "y", 0, 3, 0), (0, "z-", 0, 1, 0), (0, "z+", 0, 2, 3),
    (0, "z-", 0, 1, 3), (0, "z+", 0, 2, 0), (0, "y", 0, 3, 1),
    (0, "z+", 0, 2, 1), (0, "y", 0, 3, 2), (0, "z-", 0, 1, 2),
]
SENDS = [
    (0, "y", 1, 4, 0), (0, "z+", 3, 5, 0), (0, "z-", 1, 6, 0),
    (0, "z+", 0, 2, 2), (0, "y", 2, 5, 3), (0, "z-", 3, 4, 1),
    (1, "z-", 0, 1, 0), (0, "y", 2, 5, 1), (0, "z+", 2, 6, 1),
    (0, "y", 1, 4, 2), (0, "z+", 3, 5, 2), (0, "z-", 4, 7, 0),
    (0, "y", 0, 3, 3), (0, "z-", 0, 1, 1), (0, "z+", 5, 7, 3),
    (1, "y", 1, 4, 0), (0, "z+", 5, 7, 1), (0, "z-", 1, 6, 2),
    "scores 0",
    (0, "y", 1, 4, 3), (0, "z+", 2, 6, 3), (0, "z-", 4, 7, 2),
    (1, "y", 0, 3, 2), (1, "z+", 0, 2, 1), (1, "z-", 0, 1, 2),
    "scores 1",
    (1, "y", 0, 3, 0), (1, "z+", 0, 2, 3), (1, "z-", 4, 7, 0),
    "scores 2", "scores 3",
    (1, "y", 0, 3, 1), (1, "z+", 0, 2, 2), (1, "z-", 0, 1, 1),
    "pass 0",
    (1, "y", 2, 5, 1), (1, "z+", 0, 2, 0), (1, "z-", 1, 6, 2),
    "pass 1",
    (1, "y", 1, 4, 2), (1, "z+", 3, 5, 0), (1, "z-", 1, 6, 0),
    "pass 2",
    (1, "y", 2, 5, 3), (1, "z+", 2, 6, 1), (1, "z-", 0, 1, 3),
    "pass 3", "weights 0",
    (1, "y", 0, 3, 3), (1, "z+", 5, 7, 1), (1, "z-", 3, 4, 1),
    "weights 1",
    (1, "y", 1, 4, 3), (1, "z+", 3, 5, 2), (1, "z-", 4, 7, 2),
    "weights 2", "result 0",
    (1, "z+", 5, 7, 3), (1, "z-", 1, 6, 3),
    "weights 3", "result 1", "result 2", "result 3",
]
GROUPS = [(0, 1), (1, 3), (3, 5), (5, 8)]


def swap_matrix():
    m = np.zeros((16, 16, 16, 16), np.float32)
    for r in range(16):
        for t in range(16):
            m[r, t, t, r] = 1
    return m.reshape(256, 256).astype(ml_dtypes.bfloat16)


def cell_matrix():
    m = np.zeros((8, 128, 8, 8, 16), np.float32)
    for r in range(8):
        for j in range(8):
            for q in range(16):
                m[r, (16 * j - 8 + q) % 128, j, r, q] = 1
    return m.reshape(1024, 1024).astype(ml_dtypes.bfloat16)


def fine_matrix():
    m = np.zeros((4, 4, 32, 4, 4, 32), np.float32)
    for i in range(4):
        for b in range(4):
            for q in range(32):
                m[i, b, q, b, i, q] = 1
    return m.reshape(512, 512).astype(ml_dtypes.bfloat16)


def dot(a, b):
    return jnp.dot(a, b, preferred_element_type=F32)


def dot_t(a, b):
    return lax.dot_general(a, b, (((1,), (1,)), ((), ())), preferred_element_type=F32)


def gather_kernel(
    tgt_hbm, arc_hbm, fin_hbm, swap_hbm, cellm_hbm, finem_hbm, rows,
    t_raw, a_raw, f_raw, swap_ref, cellm, finem, ga, gf, tf, zbuf, own, xs, xr, relay, wts, inv, res,
    lsem, gsend, grecv, xsend, xrecv, rsend, rrecv,
):
    d = lax.axis_index("days")
    s = lax.axis_index("space")
    z, y = d // 2, d % 2
    partner = 2 * z + 1 - y
    to = {"y": partner, "z+": 2 * lax.rem(z + 1, 4) + y, "z-": 2 * lax.rem(z + 3, 4) + y}

    up_direct = (s != 7) & (s != 15)
    down_direct = (s != 0) & (s != 8)
    is_edge = (s == 7) | (s == 8)
    low = s < 8
    is_relay = (low & (s % 2 == 1)) | (jnp.logical_not(low) & (s % 2 == 0))
    relay_to = jnp.where(low, 8, 7)
    relay_from = jnp.where(low, 7, 8)
    quarter = (s % 8) // 2
    first_relay = jnp.where(low, 1, 8)
    last_relay = jnp.where(low, 8, 1)

    loads = [
        pltpu.make_async_copy(src, dst, lsem.at[i])
        for i, (src, dst) in enumerate(
            [
                (arc_hbm, a_raw), (swap_hbm, swap_ref), (cellm_hbm, cellm),
                (finem_hbm, finem), (fin_hbm, f_raw), (tgt_hbm, t_raw),
            ]
        )
    ]
    for load in loads:
        load.start()

    barrier = pltpu.get_barrier_semaphore()

    def greet(day, space):
        pl.semaphore_signal(barrier, inc=1, device_id=(day, space), device_id_type=MESH)

    for link in to:
        greet(to[link], s)

    @pl.when(up_direct)
    def _():
        greet(d, s + 1)

    @pl.when(down_direct)
    def _():
        greet(d, s - 1)

    @pl.when(is_relay)
    def _():
        greet(partner, relay_from)

    @pl.when(is_edge)
    def _():
        for p in range(4):
            greet(partner, last_relay + 2 * p)

    lane = lax.broadcasted_iota(jnp.int32, (1, 128), 1) % 16
    right_half = jnp.where(lane >= 8, 1.0, 0.0).astype(BF16)
    left_half = jnp.where(lane < 8, 1.0, 0.0).astype(BF16)

    def cell_rows(src, first):
        for tb in range(3):
            for cp in range(2):
                x = jnp.concatenate(
                    [src[pl.ds(first + 16 * tb, 16), 2 * cp + c].reshape(256, 128) for c in range(2)], axis=1
                )
                w = dot(swap_ref[...], x).astype(BF16)
                for c in range(2):
                    for r in range(16):
                        row = ((2 * cp + c) * 2 + r // 8) * NA + 16 * tb
                        zbuf[pl.ds(row, 16), pl.ds((r % 8) * 128, 128)] = w[16 * r : 16 * r + 16, 128 * c : 128 * c + 128]

    def supercells(jp, put):
        o = dot(zbuf[...], cellm[:, pl.ds(256 * jp, 256)]).astype(BF16)
        for c in range(4):
            for half in range(2):
                row = (2 * c + half) * NA
                for jj in range(2):
                    put(half, 2 * jp + jj, c, o[row : row + NA, 128 * jj : 128 * jj + 128])

    bufs = (ga, gf)
    wide = (4, 2)

    def piece(arr, slot, p):
        return bufs[arr].at[pl.ds(wide[arr] * p, wide[arr]), pl.ds(slot * NA, NA)]

    def remote(arr, link, src, dst, p):
        return pltpu.make_async_remote_copy(
            src_ref=piece(arr, src, p), dst_ref=piece(arr, dst, p),
            send_sem=gsend.at[arr, dst, p], recv_sem=grecv.at[arr, dst, p],
            device_id=(to[link], s), device_id_type=MESH,
        )

    arrived = {(arr, 0, p) for arr in range(2) for p in range(4)}
    sent = []

    def need(arr, slot, p):
        if (arr, slot, p) not in arrived:
            arrived.add((arr, slot, p))
            remote(arr, "y", slot, slot, p).wait_recv()

    def send(arr, link, src, dst, p):
        need(arr, src, p)
        copy = remote(arr, link, src, dst, p)
        copy.start()
        sent.append(copy)

    def blocks_of(k):
        return pl.ds(GROUPS[k][0], GROUPS[k][1] - GROUPS[k][0])

    def halo(row, k):
        there = s + 1 if row == 0 else s - 1
        return pltpu.make_async_remote_copy(
            src_ref=xs.at[row, blocks_of(k)], dst_ref=xr.at[row, blocks_of(k)],
            send_sem=xsend.at[row, k, 0], recv_sem=xrecv.at[row, k, 0],
            device_id=(d, there), device_id_type=MESH,
        )

    def halo_quarter(row, k, p):
        return pltpu.make_async_remote_copy(
            src_ref=xs.at[row, blocks_of(k), pl.ds(NA * p, NA)], dst_ref=relay.at[blocks_of(k)],
            send_sem=xsend.at[row, k, p], recv_sem=rrecv.at[k],
            device_id=(partner, first_relay + 2 * p), device_id_type=MESH,
        )

    def pass_on(row, k, p):
        if not isinstance(p, int):
            first = pl.multiple_of(NA * p, NA)
        else:
            first = NA * p
        return pltpu.make_async_remote_copy(
            src_ref=relay.at[blocks_of(k)], dst_ref=xr.at[row, blocks_of(k), pl.ds(first, NA)],
            send_sem=rsend.at[k], recv_sem=xrecv.at[row, k, p],
            device_id=(partner, relay_to), device_id_type=MESH,
        )

    def halo_start(k):
        for row, direct, edge in ((0, up_direct, 7), (1, down_direct, 8)):
            @pl.when(direct)
            def _():
                halo(row, k).start()

            @pl.when(s == edge)
            def _():
                for p in range(4):
                    halo_quarter(row, k, p).start()

    def halo_pass(k):
        for row in range(2):
            @pl.when(is_relay & (low if row == 0 else jnp.logical_not(low)))
            def _():
                halo_quarter(row, k, 0).wait_recv()
                pass_on(row, k, quarter).start()

    def halo_wait(k):
        for row, direct, edge in ((0, down_direct, 8), (1, up_direct, 7)):
            @pl.when(direct)
            def _():
                halo(row, k).wait_recv()

            @pl.when(s == edge)
            def _():
                for p in range(4):
                    pass_on(row, k, p).wait_recv()

    def halo_drain(k):
        for row, direct, edge in ((0, up_direct, 7), (1, down_direct, 8)):
            @pl.when(direct)
            def _():
                halo(row, k).wait_send()

            @pl.when(s == edge)
            def _():
                for p in range(4):
                    halo_quarter(row, k, p).wait_send()

        @pl.when(is_relay)
        def _():
            pass_on(0, k, quarter).wait_send()

    def scores(k):
        for slot in range(8):
            need(0, slot, k)

        @pl.loop(*GROUPS[k])
        def _(b):
            after = lax.rem(b + 1, NB)
            upper = dot_t(tf[b], ga[2 * b]) + dot_t(tf[b + 1], ga[2 * after])
            lower = dot_t(tf[9 + b], ga[2 * b + 1]) + dot_t(tf[10 + b], ga[2 * after + 1])
            own[b] = upper + lower
            xs[0, b] = lower
            xs[1, b] = upper

        halo_start(k)

    def weights(k):
        halo_wait(k)

        @pl.loop(*GROUPS[k])
        def _(b):
            for n in range(2):
                days = pl.ds(96 * n, 96)
                x = (own[b, days] + xr[0, b, days] + xr[1, b, days]) * (1.0 / 32.0)
                e = jnp.exp(x - jnp.max(x, axis=1, keepdims=True))
                wts[b, days] = e.astype(BF16)
                inv[b, days] = jnp.broadcast_to(1.0 / jnp.sum(e, axis=1, keepdims=True), (96, 128))

    def result(p):
        for slot in range(8):
            need(1, slot, p)

        @pl.loop(2 * p, 2 * p + 2)
        def _(b):
            scale = jnp.concatenate([inv[b], inv[b]], axis=1)
            for n in range(4):
                cols = pl.ds(256 * n, 256)
                res[b, :, cols] = (dot(wts[b], gf[b, :, cols]) * scale).astype(BF16)

        if p % 2:
            side = p // 2
            for g in range(8):
                x = jnp.concatenate([res[4 * side + b, :, pl.ds(128 * g, 128)] for b in range(4)], axis=1)
                o = dot(x, finem[...]).astype(BF16)
                for i in range(4):
                    rows[4 * g + i, :, pl.ds(128 * side, 128)] = o[:, 128 * i : 128 * i + 128]

    def put_archive(half, j, c, v):
        ga[2 * j + half, pl.ds(0, NA), pl.ds(128 * c, 128)] = v

    loads[0].wait()
    loads[1].wait()
    cell_rows(a_raw, 0)
    loads[2].wait()
    supercells(0, put_archive)
    pl.semaphore_wait(
        barrier,
        3 + up_direct.astype(jnp.int32) + down_direct.astype(jnp.int32)
        + is_relay.astype(jnp.int32) + 4 * is_edge.astype(jnp.int32),
    )
    laid = {0}
    for item in HEAD:
        if item[4] not in laid:
            laid.add(item[4])
            supercells(item[4], put_archive)
        send(*item)

    loads[3].wait()
    loads[4].wait()
    for tb in range(3):
        for half in range(2):
            x = f_raw[pl.ds(16 * tb, 16), pl.ds(16 * half, 16)].reshape(256, 256)
            w = dot(swap_ref[...], x).astype(BF16)
            for r in range(16):
                g, i = (16 * half + r) // 4, r % 4
                for side in range(2):
                    zbuf[pl.ds(NA * g + 16 * tb, 16), pl.ds(512 * side + 128 * i, 128)] = w[
                        16 * r : 16 * r + 16, 128 * side : 128 * side + 128
                    ]
    for side in range(2):
        o = dot(zbuf[:, pl.ds(512 * side, 512)], finem[...]).astype(BF16)
        for b in range(4):
            for g in range(8):
                gf[4 * side + b, pl.ds(0, NA), pl.ds(128 * g, 128)] = o[NA * g : NA * g + NA, 128 * b : 128 * b + 128]

    loads[5].wait()

    def targets(lo, hi):
        @pl.loop(lo, hi)
        def _(n):
            first = pl.multiple_of(n * NA, NA)
            days = pl.ds(first, NA)

            def put(half, j, c, v):
                cols = pl.ds(128 * c, 128)
                if j:
                    tf[9 * half + j, days, cols] = v
                else:
                    tf[9 * half, days, cols] = v * right_half
                    tf[9 * half + 8, days, cols] = v * left_half

            cell_rows(t_raw, first)
            for jp in range(4):
                supercells(jp, put)

    targets(0, 2)
    for item in SENDS[:6]:
        send(*item)
    targets(2, 4)

    for row, edge in ((0, 0), (1, 15)):
        @pl.when(s == edge)
        def _():
            xr[row] = jnp.zeros(xr.shape[1:], F32)

    todo = {"scores": scores, "pass": halo_pass, "weights": weights, "result": result}
    for item in SENDS[6:]:
        if isinstance(item, str):
            name, k = item.split()
            todo[name](int(k))
        else:
            send(*item)

    for k in range(4):
        halo_drain(k)
    for copy in sent:
        copy.wait_send()


def lay_out_kernel(rows_ref, swap_ref, out_ref):
    for tb in range(6):
        for half in range(2):
            x = rows_ref[pl.ds(16 * half, 16), pl.ds(16 * tb, 16)].reshape(256, 256)
            o = dot(swap_ref[...], x).astype(BF16)
            out_ref[pl.ds(16 * tb, 16), pl.ds(16 * half, 16)] = o.reshape(16, 16, 256)


def on_device(targets, archive, archive_fine):
    swap = jnp.asarray(swap_matrix())
    cellm = jnp.asarray(cell_matrix())
    finem = jnp.asarray(fine_matrix())
    hbm = pl.BlockSpec(memory_space=pl.ANY)
    vmem = pl.BlockSpec(memory_space=pltpu.VMEM)
    dma = pltpu.SemaphoreType.DMA
    rows = pl.pallas_call(
        gather_kernel,
        out_shape=pltpu.VMEM((32, NT, 256), BF16),
        in_specs=[hbm] * 6,
        out_specs=vmem,
        scratch_shapes=[
            pltpu.VMEM((NT, 4, 16, 128), BF16),
            pltpu.VMEM((NA, 4, 16, 128), BF16),
            pltpu.VMEM((NA, 32, 256), BF16),
            pltpu.VMEM((256, 256), BF16),
            pltpu.VMEM((1024, 1024), BF16),
            pltpu.VMEM((512, 512), BF16),
            pltpu.VMEM((16, ALL, 512), BF16),
            pltpu.VMEM((NB, ALL, 1024), BF16),
            pltpu.VMEM((18, NT, 512), BF16),
            pltpu.VMEM((8 * NA, 1024), BF16),
            pltpu.VMEM((NB, NT, ALL), F32),
            pltpu.VMEM((2, NB, NT, ALL), F32),
            pltpu.VMEM((2, NB, NT, ALL), F32),
            pltpu.VMEM((NB, NA, ALL), F32),
            pltpu.VMEM((NB, NT, ALL), BF16),
            pltpu.VMEM((NB, NT, 128), F32),
            pltpu.VMEM((NB, NT, 1024), BF16),
            dma((6,)), dma((2, 8, 4)), dma((2, 8, 4)),
            dma((2, 4, 4)), dma((2, 4, 4)), dma((4,)), dma((4,)),
        ],
        compiler_params=pltpu.CompilerParams(
            collective_id=0, has_side_effects=True, vmem_limit_bytes=56 << 20
        ),
        cost_estimate=pl.CostEstimate(flops=6_000_000_000, bytes_accessed=16_000_000, transcendentals=600_000),
    )(*[
        pltpu.with_memory_space_constraint(x, pltpu.HBM)
        for x in (targets, archive, archive_fine, swap, cellm, finem)
    ])
    return pl.pallas_call(
        lay_out_kernel,
        grid=(NT // 96,),
        out_shape=jax.ShapeDtypeStruct((NT, 32, 256), BF16),
        in_specs=[
            pl.BlockSpec((32, 96, 256), lambda n: (0, n, 0)),
            pl.BlockSpec((256, 256), lambda n: (0, 0)),
        ],
        out_specs=pl.BlockSpec((96, 32, 256), lambda n: (n, 0, 0)),
        compiler_params=pltpu.CompilerParams(vmem_limit_bytes=32 << 20),
        cost_estimate=pl.CostEstimate(flops=800_000_000, bytes_accessed=6_300_000, transcendentals=0),
    )(rows, swap)


def solution(mesh):
    return jax.shard_map(
        on_device,
        mesh=mesh,
        in_specs=(
            P("days", None, "space", None),
            P("days", None, "space", None),
            P("days", "space", None),
        ),
        out_specs=P("days", "space", None),
        check_vma=False,
    )
```

time: 108 us -> 96.4 us (0.89); the launches traced: 106 us -> 95.6 us
  Pallas kernels: 104 us -> 95.6 us
  local copies, waits for them, and re-layouts: 1.89 us -> 0.01 us
    pallas_call x2, Pallas kernels: 104 us -> 95.6 us  [the longest x1 93 us: on_device(): pl.pallas_call(gather_kernel, out_shape=pltpu.VMEM((32, NT, 256), BF16),...]
    unnamed x6 -> x2, local copies, waits for them, and re-layouts: 1.89 us -> 0.01 us
where the time goes in v2:
time: 96.4 us; the launch traced here: 95.6 us
  Pallas kernels  95.6 us (99%)
    pallas_call x1, Pallas kernels, on_device(): pl.pallas_call(gather_kernel, out_shape=pltpu.VMEM((32, NT, 256), BF16),...  93 us
    pallas_call x1, Pallas kernels, on_device(): pl.pallas_call(lay_out_kernel, grid=(NT // 96,), out_shape=jax.ShapeDtype...  2.55 us

profile of v2, /device:TPU:1, one launch (start us, length us, event | category | flops | bytes accessed | tf_op | source)
XLA Modules:
  0.0 95.6 jit_solution(1238501841212277688)
XLA Ops:
  0.0 0.0 copy-start
  0.0 93.0 %shard_map.64.rows_ref = bf16[32,192,256]{2,1,0:T(8,128)(2,1)S(1)} custom-call(bf16[192,4,16,128]{3,2,1,0:T(8,128)(2,1)} %tgt_hbm.1, bf16[48,4,16,128]{3,2,1,0:T(8,128)(2,1)} %arc_hbm.1, bf16[48,32,256]{2,1,0:T(8,128)(2,1)} %fin_hbm.1, bf16[256,256]{1,0:T(8,128)(2,1)} %constant.6.clone.swap_hbm.swap_ref, bf16[1024,1024]{1,0:T(8,128)(2,1)} %constant.7.clone.cellm_hbm, ...), custom_call_target="tpu_custom_call" | custom-call | flops 6000000000 | bytes 16000000 | tf_op jit(solution)/shard_map/pallas_call | solution.py:414
  93.0 0.0 copy-done
  93.0 2.6 %shard_map.65 = bf16[192,32,256]{2,1,0:T(8,128)(2,1)} custom-call(bf16[32,192,256]{2,1,0:T(8,128)(2,1)S(1)} %shard_map.64.rows_ref, bf16[256,256]{1,0:T(8,128)(2,1)S(1)} %copy-done), custom_call_target="tpu_custom_call" | custom-call | flops 800000000 | bytes 6300000 | tf_op jit(solution)/shard_map/pallas_call | solution.py:448
Async XLA Ops:
  0.0 93.0 %copy-start = (bf16[256,256]{1,0:T(8,128)(2,1)S(1)}, bf16[256,256]{1,0:T(8,128)(2,1)}, u32[]{:S(2)}) copy-start(bf16[256,256]{1,0:T(8,128)(2,1)} %constant.6.clone.swap_hbm.swap_ref) | copy-start | bytes 393220

commit v3 on v2

--- a/solution.py
+++ b/solution.py
@@ -16,37 +16,22 @@
 ALL = 8 * NA
 
 HEAD = [
-    (0, "y", 0, 3, 0), (0, "z-", 0, 1, 0), (0, "z+", 0, 2, 3),
-    (0, "z-", 0, 1, 3), (0, "z+", 0, 2, 0), (0, "y", 0, 3, 1),
-    (0, "z+", 0, 2, 1), (0, "y", 0, 3, 2), (0, "z-", 0, 1, 2),
+    (0, "y", 0, 3, 0), (0, "z+", 0, 2, 1), (0, "z-", 0, 1, 0), (0, "y", 0, 3, 1), (0, "z+", 0, 2, 0),
+    (0, "z-", 0, 1, 2), (0, "y", 1, 4, 0), (0, "z+", 0, 2, 3), (0, "z-", 1, 6, 0),
 ]
 SENDS = [
-    (0, "y", 1, 4, 0), (0, "z+", 3, 5, 0), (0, "z-", 1, 6, 0),
-    (0, "z+", 0, 2, 2), (0, "y", 2, 5, 3), (0, "z-", 3, 4, 1),
-    (1, "z-", 0, 1, 0), (0, "y", 2, 5, 1), (0, "z+", 2, 6, 1),
-    (0, "y", 1, 4, 2), (0, "z+", 3, 5, 2), (0, "z-", 4, 7, 0),
-    (0, "y", 0, 3, 3), (0, "z-", 0, 1, 1), (0, "z+", 5, 7, 3),
-    (1, "y", 1, 4, 0), (0, "z+", 5, 7, 1), (0, "z-", 1, 6, 2),
-    "scores 0",
-    (0, "y", 1, 4, 3), (0, "z+", 2, 6, 3), (0, "z-", 4, 7, 2),
-    (1, "y", 0, 3, 2), (1, "z+", 0, 2, 1), (1, "z-", 0, 1, 2),
-    "scores 1",
-    (1, "y", 0, 3, 0), (1, "z+", 0, 2, 3), (1, "z-", 4, 7, 0),
-    "scores 2", "scores 3",
-    (1, "y", 0, 3, 1), (1, "z+", 0, 2, 2), (1, "z-", 0, 1, 1),
-    "pass 0",
-    (1, "y", 2, 5, 1), (1, "z+", 0, 2, 0), (1, "z-", 1, 6, 2),
-    "pass 1",
-    (1, "y", 1, 4, 2), (1, "z+", 3, 5, 0), (1, "z-", 1, 6, 0),
-    "pass 2",
-    (1, "y", 2, 5, 3), (1, "z+", 2, 6, 1), (1, "z-", 0, 1, 3),
-    "pass 3", "weights 0",
-    (1, "y", 0, 3, 3), (1, "z+", 5, 7, 1), (1, "z-", 3, 4, 1),
-    "weights 1",
-    (1, "y", 1, 4, 3), (1, "z+", 3, 5, 2), (1, "z-", 4, 7, 2),
-    "weights 2", "result 0",
-    (1, "z+", 5, 7, 3), (1, "z-", 1, 6, 3),
-    "weights 3", "result 1", "result 2", "result 3",
+    (0, "y", 2, 5, 1), (0, "z+", 3, 5, 0), (0, "z-", 0, 1, 1), (0, "y", 0, 3, 2), (0, "z+", 2, 6, 1),
+    (0, "z-", 4, 7, 0), (0, "y", 1, 4, 2), (0, "z+", 5, 7, 1), (1, "z-", 0, 1, 0), (0, "z-", 3, 4, 1),
+    "scores 0", (1, "y", 0, 3, 0), (1, "z+", 0, 2, 1), (0, "y", 2, 5, 3), (0, "z-", 0, 1, 3),
+    (0, "z+", 0, 2, 2), "scores 1", (0, "z-", 1, 6, 2), (1, "y", 1, 4, 0), (0, "z+", 3, 5, 2), "pass 0",
+    (0, "z-", 4, 7, 2), (0, "y", 0, 3, 3), (0, "z+", 2, 6, 3), (1, "z-", 1, 6, 0), "pass 1", (0, "y", 1, 4, 3),
+    (0, "z+", 5, 7, 3), "scores 2", (1, "z-", 4, 7, 0), (1, "y", 0, 3, 1), (1, "z+", 0, 2, 0),
+    (1, "z+", 0, 2, 3), (1, "z-", 0, 1, 2), "weights 0", "scores 3", "lay 2", (1, "y", 2, 5, 1),
+    (1, "z+", 3, 5, 0), (1, "z-", 0, 1, 1), "weights 1", "lay 3", "pass 2", (1, "z+", 2, 6, 1),
+    (1, "z-", 3, 4, 1), (1, "y", 1, 4, 2), "lay 1", "lay 5", (1, "z+", 5, 7, 1), (1, "z-", 0, 1, 3), "pass 3",
+    (1, "y", 0, 3, 2), "lay 4", "lay 6", (1, "z+", 0, 2, 2), (1, "z-", 1, 6, 2), (1, "y", 2, 5, 3), "lay 7",
+    "result 0", "weights 2", "result 1", (1, "z-", 4, 7, 2), (1, "z+", 3, 5, 2), (1, "y", 0, 3, 3),
+    (1, "z-", 1, 6, 3), (1, "z+", 5, 7, 3), (1, "y", 1, 4, 3), "weights 3", "result 2", "result 3",
 ]
 GROUPS = [(0, 1), (1, 3), (3, 5), (5, 8)]
 
@@ -87,8 +72,8 @@
 
 def gather_kernel(
     tgt_hbm, arc_hbm, fin_hbm, swap_hbm, cellm_hbm, finem_hbm, rows,
-    t_raw, a_raw, f_raw, swap_ref, cellm, finem, ga, gf, tf, zbuf, own, xs, xr, relay, wts, inv, res,
-    lsem, gsend, grecv, xsend, xrecv, rsend, rrecv,
+    t_raw, a_raw, f_raw, f_left, swap_ref, cellm, finem, ga, gf, tf, zbuf, own, xs, xr, relay, wts, inv, res,
+    lsem, gsend, grecv, xsend, xrecv, rsend, rrecv, esend, erecv,
 ):
     d = lax.axis_index("days")
     s = lax.axis_index("space")
@@ -112,7 +97,12 @@
         for i, (src, dst) in enumerate(
             [
                 (arc_hbm, a_raw), (swap_hbm, swap_ref), (cellm_hbm, cellm),
-                (finem_hbm, finem), (fin_hbm, f_raw), (tgt_hbm, t_raw),
+                (finem_hbm, finem),
+                (fin_hbm.at[:, pl.ds(0, 16), pl.ds(0, 128)], f_left.at[0, 0]),
+                (fin_hbm.at[:, pl.ds(16, 16), pl.ds(0, 128)], f_left.at[1, 0]),
+                (fin_hbm.at[:, pl.ds(0, 16), pl.ds(128, 128)], f_raw.at[0]),
+                (fin_hbm.at[:, pl.ds(16, 16), pl.ds(128, 128)], f_raw.at[1]),
+                (tgt_hbm, t_raw),
             ]
         )
     ]
@@ -172,12 +162,24 @@
     wide = (4, 2)
 
     def piece(arr, slot, p):
+        if arr == 1 and p < 2:
+            return f_left.at[p, slot]
         return bufs[arr].at[pl.ds(wide[arr] * p, wide[arr]), pl.ds(slot * NA, NA)]
 
     def remote(arr, link, src, dst, p):
+        mine, there = piece(arr, src, p), piece(arr, dst, p)
+        if arr == 1 and p == 0 and dst < 4:
+            mine, there = mine.at[pl.ds(32, 16)], there.at[pl.ds(32, 16)]
         return pltpu.make_async_remote_copy(
-            src_ref=piece(arr, src, p), dst_ref=piece(arr, dst, p),
+            src_ref=mine, dst_ref=there,
             send_sem=gsend.at[arr, dst, p], recv_sem=grecv.at[arr, dst, p],
+            device_id=(to[link], s), device_id_type=MESH,
+        )
+
+    def early(link, dst):
+        return pltpu.make_async_remote_copy(
+            src_ref=fin_hbm.at[pl.ds(0, 32), pl.ds(0, 16), pl.ds(0, 128)], dst_ref=f_left.at[0, dst, pl.ds(0, 32)],
+            send_sem=esend.at[dst], recv_sem=erecv.at[dst],
             device_id=(to[link], s), device_id_type=MESH,
         )
 
@@ -188,6 +190,8 @@
         if (arr, slot, p) not in arrived:
             arrived.add((arr, slot, p))
             remote(arr, "y", slot, slot, p).wait_recv()
+            if arr == 1 and p == 0 and slot < 4:
+                early("y", slot).wait_recv()
 
     def send(arr, link, src, dst, p):
         need(arr, src, p)
@@ -295,9 +299,34 @@
                 wts[b, days] = e.astype(BF16)
                 inv[b, days] = jnp.broadcast_to(1.0 / jnp.sum(e, axis=1, keepdims=True), (96, 128))
 
+    def fine_blocks(src, side, slot):
+        for tb in range(3):
+            x = jnp.concatenate(
+                [src[half, pl.ds(16 * tb, 16)].reshape(256, 128) for half in range(2)], axis=1
+            )
+            w = dot(swap_ref[...], x).astype(BF16)
+            for half in range(2):
+                for r in range(16):
+                    g, i = (16 * half + r) // 4, r % 4
+                    zbuf[pl.ds(NA * g + 16 * tb, 16), pl.ds(128 * i, 128)] = w[
+                        16 * r : 16 * r + 16, 128 * half : 128 * half + 128
+                    ]
+        o = dot(zbuf[:, pl.ds(0, 512)], finem[...]).astype(BF16)
+        for b in range(4):
+            for g in range(8):
+                gf[4 * side + b, pl.ds(NA * slot, NA), pl.ds(128 * g, 128)] = o[
+                    NA * g : NA * g + NA, 128 * b : 128 * b + 128
+                ]
+
+    def lay(slot):
+        need(1, slot, 0)
+        need(1, slot, 1)
+        fine_blocks(f_left.at[:, slot], 0, slot)
+
     def result(p):
-        for slot in range(8):
-            need(1, slot, p)
+        if p > 1:
+            for slot in range(8):
+                need(1, slot, p)
 
         @pl.loop(2 * p, 2 * p + 2)
         def _(b):
@@ -306,53 +335,48 @@
                 cols = pl.ds(256 * n, 256)
                 res[b, :, cols] = (dot(wts[b], gf[b, :, cols]) * scale).astype(BF16)
 
-        if p % 2:
-            side = p // 2
-            for g in range(8):
-                x = jnp.concatenate([res[4 * side + b, :, pl.ds(128 * g, 128)] for b in range(4)], axis=1)
-                o = dot(x, finem[...]).astype(BF16)
-                for i in range(4):
-                    rows[4 * g + i, :, pl.ds(128 * side, 128)] = o[:, 128 * i : 128 * i + 128]
+        side = p // 2
+        for g in range(8):
+            x = jnp.concatenate([res[2 * p + b, :, pl.ds(128 * g, 128)] for b in range(2)], axis=1)
+            o = dot(x, finem[pl.ds(256 * (p % 2), 256)]).astype(BF16)
+            for i in range(4):
+                v = o[:, 128 * i : 128 * i + 128]
+                if p % 2:
+                    v = v + rows[4 * g + i, :, pl.ds(128 * side, 128)]
+                rows[4 * g + i, :, pl.ds(128 * side, 128)] = v
 
     def put_archive(half, j, c, v):
         ga[2 * j + half, pl.ds(0, NA), pl.ds(128 * c, 128)] = v
 
-    loads[0].wait()
-    loads[1].wait()
-    cell_rows(a_raw, 0)
-    loads[2].wait()
-    supercells(0, put_archive)
     pl.semaphore_wait(
         barrier,
         3 + up_direct.astype(jnp.int32) + down_direct.astype(jnp.int32)
         + is_relay.astype(jnp.int32) + 4 * is_edge.astype(jnp.int32),
     )
-    laid = {0}
+    for link, dst in (("y", 3), ("z+", 2), ("z-", 1)):
+        copy = early(link, dst)
+        copy.start()
+        sent.append(copy)
+    loads[0].wait()
+    loads[1].wait()
+    cell_rows(a_raw, 0)
+    loads[2].wait()
+    laid = set()
     for item in HEAD:
         if item[4] not in laid:
             laid.add(item[4])
             supercells(item[4], put_archive)
         send(*item)
-
-    loads[3].wait()
-    loads[4].wait()
-    for tb in range(3):
-        for half in range(2):
-            x = f_raw[pl.ds(16 * tb, 16), pl.ds(16 * half, 16)].reshape(256, 256)
-            w = dot(swap_ref[...], x).astype(BF16)
-            for r in range(16):
-                g, i = (16 * half + r) // 4, r % 4
-                for side in range(2):
-                    zbuf[pl.ds(NA * g + 16 * tb, 16), pl.ds(512 * side + 128 * i, 128)] = w[
-                        16 * r : 16 * r + 16, 128 * side : 128 * side + 128
-                    ]
-    for side in range(2):
-        o = dot(zbuf[:, pl.ds(512 * side, 512)], finem[...]).astype(BF16)
-        for b in range(4):
-            for g in range(8):
-                gf[4 * side + b, pl.ds(0, NA), pl.ds(128 * g, 128)] = o[NA * g : NA * g + NA, 128 * b : 128 * b + 128]
-
-    loads[5].wait()
+    for p in range(4):
+        if p not in laid:
+            supercells(p, put_archive)
+
+    for load in loads[3:8]:
+        load.wait()
+    fine_blocks(f_left.at[:, 0], 0, 0)
+    fine_blocks(f_raw, 1, 0)
+
+    loads[8].wait()
 
     def targets(lo, hi):
         @pl.loop(lo, hi)
@@ -382,7 +406,7 @@
         def _():
             xr[row] = jnp.zeros(xr.shape[1:], F32)
 
-    todo = {"scores": scores, "pass": halo_pass, "weights": weights, "result": result}
+    todo = {"scores": scores, "pass": halo_pass, "weights": weights, "lay": lay, "result": result}
     for item in SENDS[6:]:
         if isinstance(item, str):
             name, k = item.split()
@@ -396,12 +420,19 @@
         copy.wait_send()
 
 
-def lay_out_kernel(rows_ref, swap_ref, out_ref):
-    for tb in range(6):
-        for half in range(2):
-            x = rows_ref[pl.ds(16 * half, 16), pl.ds(16 * tb, 16)].reshape(256, 256)
-            o = dot(swap_ref[...], x).astype(BF16)
-            out_ref[pl.ds(16 * tb, 16), pl.ds(16 * half, 16)] = o.reshape(16, 16, 256)
+def lay_out_kernel(rows_ref, swap_ref, out_hbm, laid, sems):
+    stores = []
+    for part in range(4):
+        for tb in range(3 * part, 3 * part + 3):
+            for half in range(2):
+                x = rows_ref[pl.ds(16 * half, 16), pl.ds(16 * tb, 16)].reshape(256, 256)
+                o = dot(swap_ref[...], x).astype(BF16)
+                laid[pl.ds(16 * tb, 16), pl.ds(16 * half, 16)] = o.reshape(16, 16, 256)
+        days = pl.ds(48 * part, 48)
+        stores.append(pltpu.make_async_copy(laid.at[days], out_hbm.at[days], sems.at[part]))
+        stores[-1].start()
+    for store in stores:
+        store.wait()
 
 
 def on_device(targets, archive, archive_fine):
@@ -419,7 +450,8 @@
         scratch_shapes=[
             pltpu.VMEM((NT, 4, 16, 128), BF16),
             pltpu.VMEM((NA, 4, 16, 128), BF16),
-            pltpu.VMEM((NA, 32, 256), BF16),
+            pltpu.VMEM((2, NA, 16, 128), BF16),
+            pltpu.VMEM((2, 8, NA, 16, 128), BF16),
             pltpu.VMEM((256, 256), BF16),
             pltpu.VMEM((1024, 1024), BF16),
             pltpu.VMEM((512, 512), BF16),
@@ -434,8 +466,8 @@
             pltpu.VMEM((NB, NT, ALL), BF16),
             pltpu.VMEM((NB, NT, 128), F32),
             pltpu.VMEM((NB, NT, 1024), BF16),
-            dma((6,)), dma((2, 8, 4)), dma((2, 8, 4)),
-            dma((2, 4, 4)), dma((2, 4, 4)), dma((4,)), dma((4,)),
+            dma((9,)), dma((2, 8, 4)), dma((2, 8, 4)),
+            dma((2, 4, 4)), dma((2, 4, 4)), dma((4,)), dma((4,)), dma((4,)), dma((4,)),
         ],
         compiler_params=pltpu.CompilerParams(
             collective_id=0, has_side_effects=True, vmem_limit_bytes=56 << 20
@@ -447,13 +479,10 @@
     ])
     return pl.pallas_call(
         lay_out_kernel,
-        grid=(NT // 96,),
         out_shape=jax.ShapeDtypeStruct((NT, 32, 256), BF16),
-        in_specs=[
-            pl.BlockSpec((32, 96, 256), lambda n: (0, n, 0)),
-            pl.BlockSpec((256, 256), lambda n: (0, 0)),
-        ],
-        out_specs=pl.BlockSpec((96, 32, 256), lambda n: (n, 0, 0)),
+        in_specs=[vmem, vmem],
+        out_specs=hbm,
+        scratch_shapes=[pltpu.VMEM((NT, 32, 256), BF16), dma((4,))],
         compiler_params=pltpu.CompilerParams(vmem_limit_bytes=32 << 20),
         cost_estimate=pl.CostEstimate(flops=800_000_000, bytes_accessed=6_300_000, transcendentals=0),
     )(rows, swap)

time: 96.4 us -> 96 us (level)
  no operation moved by 1% of the time
where the time goes in v3:
time: 96 us; the launch traced here: 95.4 us
  Pallas kernels  95.2 us (99%)
    pallas_call x1, Pallas kernels, on_device(): pl.pallas_call(gather_kernel, out_shape=pltpu.VMEM((32, NT, 256), BF16),...  93.2 us
    pallas_call x1, Pallas kernels, on_device(): pl.pallas_call(lay_out_kernel, out_shape=jax.ShapeDtypeStruct((NT, 32, 25...  2.07 us

profile of v3, /device:TPU:1, one launch (start us, length us, event | category | flops | bytes accessed | tf_op | source)
XLA Modules:
  0.0 95.4 jit_solution(18352898892536599372)
XLA Ops:
  0.0 0.0 copy-start
  0.0 93.2 %shard_map.64.rows_ref = bf16[32,192,256]{2,1,0:T(8,128)(2,1)S(1)} custom-call(bf16[192,4,16,128]{3,2,1,0:T(8,128)(2,1)} %tgt_hbm.1, bf16[48,4,16,128]{3,2,1,0:T(8,128)(2,1)} %arc_hbm.1, bf16[48,32,256]{2,1,0:T(8,128)(2,1)} %fin_hbm.1, bf16[256,256]{1,0:T(8,128)(2,1)} %constant.6.clone.swap_hbm.swap_ref, bf16[1024,1024]{1,0:T(8,128)(2,1)} %constant.7.clone.cellm_hbm, ...), custom_call_target="tpu_custom_call" | custom-call | flops 6000000000 | bytes 16000000 | tf_op jit(solution)/shard_map/pallas_call | solution.py:445
  93.2 0.0 copy-done
  93.2 2.1 %shard_map.65 = bf16[192,32,256]{2,1,0:T(8,128)(2,1)} custom-call(bf16[32,192,256]{2,1,0:T(8,128)(2,1)S(1)} %shard_map.64.rows_ref, bf16[256,256]{1,0:T(8,128)(2,1)S(1)} %copy-done), custom_call_target="tpu_custom_call" | custom-call | flops 800000000 | bytes 6300000 | tf_op jit(solution)/shard_map/pallas_call | solution.py:480
Async XLA Ops:
  0.0 93.2 %copy-start = (bf16[256,256]{1,0:T(8,128)(2,1)S(1)}, bf16[256,256]{1,0:T(8,128)(2,1)}, u32[]{:S(2)}) copy-start(bf16[256,256]{1,0:T(8,128)(2,1)} %constant.6.clone.swap_hbm.swap_ref) | copy-start | bytes 393220

commit v4 on v3

--- a/solution.py
+++ b/solution.py
@@ -26,10 +26,10 @@
     (0, "z+", 0, 2, 2), "scores 1", (0, "z-", 1, 6, 2), (1, "y", 1, 4, 0), (0, "z+", 3, 5, 2), "pass 0",
     (0, "z-", 4, 7, 2), (0, "y", 0, 3, 3), (0, "z+", 2, 6, 3), (1, "z-", 1, 6, 0), "pass 1", (0, "y", 1, 4, 3),
     (0, "z+", 5, 7, 3), "scores 2", (1, "z-", 4, 7, 0), (1, "y", 0, 3, 1), (1, "z+", 0, 2, 0),
-    (1, "z+", 0, 2, 3), (1, "z-", 0, 1, 2), "weights 0", "scores 3", "lay 2", (1, "y", 2, 5, 1),
-    (1, "z+", 3, 5, 0), (1, "z-", 0, 1, 1), "weights 1", "lay 3", "pass 2", (1, "z+", 2, 6, 1),
-    (1, "z-", 3, 4, 1), (1, "y", 1, 4, 2), "lay 1", "lay 5", (1, "z+", 5, 7, 1), (1, "z-", 0, 1, 3), "pass 3",
-    (1, "y", 0, 3, 2), "lay 4", "lay 6", (1, "z+", 0, 2, 2), (1, "z-", 1, 6, 2), (1, "y", 2, 5, 3), "lay 7",
+    (1, "z+", 0, 2, 3), (1, "z-", 0, 1, 2), "scores 3", (1, "y", 2, 5, 1), "lay 2", (1, "z+", 3, 5, 0),
+    (1, "z-", 0, 1, 1), "weights 0", "lay 3", "pass 2", (1, "z+", 2, 6, 1), (1, "z-", 3, 4, 1),
+    (1, "y", 1, 4, 2), "weights 1", "lay 1", (1, "z+", 5, 7, 1), "lay 5", (1, "z-", 0, 1, 3), "pass 3",
+    (1, "y", 0, 3, 2), (1, "z+", 0, 2, 2), "lay 4", "lay 6", (1, "z-", 1, 6, 2), (1, "y", 2, 5, 3), "lay 7",
     "result 0", "weights 2", "result 1", (1, "z-", 4, 7, 2), (1, "z+", 3, 5, 2), (1, "y", 0, 3, 3),
     (1, "z-", 1, 6, 3), (1, "z+", 5, 7, 3), (1, "y", 1, 4, 3), "weights 3", "result 2", "result 3",
 ]

time: 96 us -> 95.2 us (level)
  no operation moved by 1% of the time
where the time goes in v4:
time: 95.2 us; the launch traced here: 95.1 us
  Pallas kernels  94.9 us (100%)
    pallas_call x1, Pallas kernels, on_device(): pl.pallas_call(gather_kernel, out_shape=pltpu.VMEM((32, NT, 256), BF16),...  92.8 us
    pallas_call x1, Pallas kernels, on_device(): pl.pallas_call(lay_out_kernel, out_shape=jax.ShapeDtypeStruct((NT, 32, 25...  2.07 us

profile of v4, /device:TPU:1, one launch (start us, length us, event | category | flops | bytes accessed | tf_op | source)
XLA Modules:
  0.0 95.1 jit_solution(8196030357057015860)
XLA Ops:
  0.0 0.0 copy-start
  0.0 92.8 %shard_map.64.rows_ref = bf16[32,192,256]{2,1,0:T(8,128)(2,1)S(1)} custom-call(bf16[192,4,16,128]{3,2,1,0:T(8,128)(2,1)} %tgt_hbm.1, bf16[48,4,16,128]{3,2,1,0:T(8,128)(2,1)} %arc_hbm.1, bf16[48,32,256]{2,1,0:T(8,128)(2,1)} %fin_hbm.1, bf16[256,256]{1,0:T(8,128)(2,1)} %constant.6.clone.swap_hbm.swap_ref, bf16[1024,1024]{1,0:T(8,128)(2,1)} %constant.7.clone.cellm_hbm, ...), custom_call_target="tpu_custom_call" | custom-call | flops 6000000000 | bytes 16000000 | tf_op jit(solution)/shard_map/pallas_call | solution.py:445
  92.9 0.0 copy-done
  92.9 2.1 %shard_map.65 = bf16[192,32,256]{2,1,0:T(8,128)(2,1)} custom-call(bf16[32,192,256]{2,1,0:T(8,128)(2,1)S(1)} %shard_map.64.rows_ref, bf16[256,256]{1,0:T(8,128)(2,1)S(1)} %copy-done), custom_call_target="tpu_custom_call" | custom-call | flops 800000000 | bytes 6300000 | tf_op jit(solution)/shard_map/pallas_call | solution.py:480
Async XLA Ops:
  0.0 92.9 %copy-start = (bf16[256,256]{1,0:T(8,128)(2,1)S(1)}, bf16[256,256]{1,0:T(8,128)(2,1)}, u32[]{:S(2)}) copy-start(bf16[256,256]{1,0:T(8,128)(2,1)} %constant.6.clone.swap_hbm.swap_ref) | copy-start | bytes 393220
